TPU v7x, 512 devices: a whole 4x4x16 slice. The times are simulated.
512 devices in a mesh: batch: 16 (over z), proto: 32 (over y, x, core).
Axes of the slice: x: 4, y: 4, z: 16, core: 2. Of those that a mesh axis runs over, the one named last changes fastest.
Arguments:
- teacher_feats: bfloat16 [4096, 256], P('batch'), may hold values from -2 to 2
- student_feats: bfloat16 [4096, 256], P('batch'), may hold values from -2 to 2
- teacher_weight: bfloat16 [256, 131072], P(None, 'proto'), may hold values from -2 to 2
- student_weight: bfloat16 [256, 131072], P(None, 'proto'), may hold values from -2 to 2
Outputs:
- weight_grad: bfloat16 [256, 131072], P('batch', 'proto')
- feature_grad: bfloat16 [4096, 256], P('batch')
All inputs are finite; a program needn't handle non-finite values.
Results may differ from a plain program's by a relative error of at most 0.025.
Values may be sent and summed in bfloat16 or wider, within the bound.
A program may use at most 64 MiB of HBM per device.

v0:
```python
import math

import jax
import jax.numpy as jnp
from jax import lax
from jax.sharding import PartitionSpec as P

ITERS = 3


teacher_temp = 0.07
student_temp = 0.1
epsilon = 1e-06


def unit_rows(raw):
    values = raw.astype(jnp.float32)
    length = jnp.sqrt(jnp.sum(values * values, axis=1, keepdims=True) + epsilon)
    return (values / length, length)


def unit_columns(raw):
    values = raw.astype(jnp.float32)
    length = jnp.sqrt(jnp.sum(values * values, axis=0, keepdims=True) + epsilon)
    return (values / length).astype(jnp.bfloat16)


def proto_update(teacher_exp, crop_scale):
    sums = lax.psum(jnp.sum(teacher_exp * crop_scale[:, None], axis=0), "batch")
    return 1.0 / sums


def through_norm(unit_grad, unit, length):
    along = jnp.sum(unit * unit_grad, axis=1, keepdims=True)
    return ((unit_grad - unit * along) / length).astype(jnp.bfloat16)


def shards(teacher_feats, student_feats, teacher_weight, student_weight):
    teacher_unit, _ = unit_rows(teacher_feats)
    teacher_half = teacher_unit.astype(jnp.bfloat16)
    student_unit, student_len = unit_rows(student_feats)
    student_half = student_unit.astype(jnp.bfloat16)
    teacher_cols = unit_columns(teacher_weight)
    student_cols = unit_columns(student_weight)
    crops_here = teacher_half.shape[0]
    width = teacher_half.shape[1]
    batch_count = lax.axis_size("batch")
    proto_count = lax.axis_size("proto")
    crops_all = crops_here * batch_count
    protos_all = teacher_cols.shape[1] * proto_count
    teacher_exp = jnp.exp(
        jnp.dot(teacher_half, teacher_cols, preferred_element_type=jnp.float32) / teacher_temp
    )
    logits = jnp.dot(student_half, student_cols, preferred_element_type=jnp.float32) / student_temp
    local_totals = jnp.sum(jnp.exp(logits), axis=1)
    crop_scale = jnp.ones((crops_here,), jnp.float32)
    for sweep_index in range(ITERS):
        proto_scale = proto_update(teacher_exp, crop_scale)
        crop_sums = lax.psum(jnp.sum(teacher_exp * proto_scale[None, :], axis=1), "proto")
        crop_scale = 1.0 / crop_sums
    student_totals = lax.psum(local_totals, "proto")
    targets = teacher_exp * proto_scale[None, :] * crop_scale[:, None]
    log_total = jnp.log(student_totals)[:, None]
    student_prob = jnp.exp(logits - log_total)
    grad_logits = (protos_all * (student_prob - targets)).astype(jnp.bfloat16)
    weight_factor = math.sqrt(width / crops_all)
    weight_term_all = (
        lax.dot_general(
            student_half, grad_logits, (((0,), (0,)), ((), ())), preferred_element_type=jnp.float32
        )
        * weight_factor
    )
    weight_part = lax.psum_scatter(
        weight_term_all.astype(jnp.bfloat16), "batch", scatter_dimension=0, tiled=True
    )
    feature_factor = math.sqrt(width / protos_all)
    local_grad = (
        lax.dot_general(
            grad_logits, student_cols, (((1,), (1,)), ((), ())), preferred_element_type=jnp.float32
        )
        * feature_factor
    )
    unit_grad = lax.psum(local_grad.astype(jnp.bfloat16), "proto").astype(jnp.float32)
    feature_grad = through_norm(unit_grad, student_unit, student_len)
    return (weight_part, feature_grad)


def solution(mesh):
    return jax.shard_map(
        shards,
        mesh=mesh,
        in_specs=(P("batch", None), P("batch", None), P(None, "proto"), P(None, "proto")),
        out_specs=(P("batch", "proto"), P("batch", None)),
        check_vma=False,
    )
```

profile of v0, /device:TPU:1, one launch (start us, length us, event | category | flops | bytes accessed | tf_op | source)
XLA Modules:
  0.0 529.4 jit_solution(6255935654761743090)
XLA Ops:
  8.0 0.0 copy-start.4
  8.0 0.0 copy-start.1
  8.0 0.0 all-reduce.3.cloned.1.call-start
  8.1 1.2 fusion.10
  9.2 1.0 fusion.9
  10.3 2.0 fusion.4
  12.3 2.0 fusion.2
  14.4 0.0 copy-done.4
  14.4 0.0 copy-done.1
  14.4 3.1 fusion.21
  17.5 49.1 %psum.57 = f32[4096]{0:T(1024)S(1)} all-reduce(f32[4096]{0:T(1024)S(1)} %get-tuple-element.4), channel_id=1, replica_groups=mesh['batch'=16,'proto'=32] {'batch'}, use_global_device_ids=true, to_apply=%region_7.0 | all-reduce | flops 4096 | bytes 32768 | tf_op jit(solution)/shard_map/psum | solution.py:29
  66.6 2.6 multiply_reduce_fusion.3
  69.2 76.7 %psum.58 = f32[256]{0:T(256)S(1)} all-reduce(f32[256]{0:T(256)S(1)} %multiply_reduce_fusion.3), channel_id=1, replica_groups=mesh['batch'=16,'proto'=32] {'proto'}, use_global_device_ids=true, to_apply=%region_9.0 | all-reduce | flops 256 | bytes 2048 | tf_op jit(solution)/shard_map/psum | solution.py:59
  145.9 2.7 multiply_reduce_fusion.2
  148.6 39.0 %psum.59 = f32[4096]{0:T(1024)S(1)} all-reduce(f32[4096]{0:T(1024)S(1)} %multiply_reduce_fusion.2), channel_id=1, replica_groups=mesh['batch'=16,'proto'=32] {'batch'}, use_global_device_ids=true, to_apply=%region_11.0 | all-reduce | flops 4096 | bytes 32768 | tf_op jit(solution)/shard_map/psum | solution.py:29
  187.6 2.6 multiply_reduce_fusion.1
  190.1 76.1 %psum.60 = f32[256]{0:T(256)S(1)} all-reduce(f32[256]{0:T(256)S(1)} %multiply_reduce_fusion.1), channel_id=1, replica_groups=mesh['batch'=16,'proto'=32] {'proto'}, use_global_device_ids=true, to_apply=%region_13.0 | all-reduce | flops 256 | bytes 2048 | tf_op jit(solution)/shard_map/psum | solution.py:59
  266.2 0.0 copy-start
  266.2 0.0 copy-start.2
  266.2 2.8 multiply_reduce_fusion
  269.1 39.2 %psum.61 = f32[4096]{0:T(1024)S(1)} all-reduce(f32[4096]{0:T(1024)S(1)} %multiply_reduce_fusion), channel_id=1, replica_groups=mesh['batch'=16,'proto'=32] {'batch'}, use_global_device_ids=true, to_apply=%region_15.0 | all-reduce | flops 4096 | bytes 32768 | tf_op jit(solution)/shard_map/psum | solution.py:29
  308.3 2.6 multiply_reduce_fusion.4
  310.9 0.0 copy-done
  310.9 0.0 copy-done.2
  310.9 3.0 exponential_reduce_fusion
  313.9 76.6 %all-reduce = (f32[256]{0:T(256)S(1)}, f32[256]{0:T(256)S(1)}) all-reduce(f32[256]{0:T(256)S(1)} %multiply_reduce_fusion.4, f32[256]{0:T(256)S(1)} %get-tuple-element.6), channel_id=1, replica_groups=mesh['batch'=16,'proto'=32] {'proto'}, use_global_device_ids=true, to_apply=%region_17.0 | all-reduce | flops 512 | bytes 4096 | tf_op jit(solution)/shard_map/psum | solution.py:59
  390.6 0.0 copy-start.3
  390.6 4.9 multiply_convert_fusion
  395.5 0.0 copy-done.3
  395.5 1.4 fusion.8
  396.9 0.0 all-reduce.3.cloned.1.call-update
  396.9 0.0 reduce-scatter.2.cloned.1.call-start
  397.0 2.2 fusion.1
  399.2 0.0 reduce-scatter.2.cloned.1.call-update
  399.2 120.0 %all-reduce.3.cloned.1.call-done = bf16[256,256]{1,0:T(8,128)(2,1)} async-done(((bf16[256,256]{1,0:T(8,128)(2,1)}), bf16[256,256]{1,0:T(8,128)(2,1)}) %all-reduce.3.cloned.1.call-update) | async-done | bytes 131088 | tf_op jit(solution)/shard_map/psum | solution.py:83
  519.2 1.1 fusion.12
  520.3 1.7 fusion.14
  522.0 0.0 reduce-scatter.2.cloned.1.call-done
  (11 shorter events, 0.1 us)
Async XLA Ops:
  8.0 6.4 %copy-start.4 = (bf16[256,256]{1,0:T(8,128)(2,1)S(1)}, bf16[256,256]{1,0:T(8,128)(2,1)}, u32[]{:S(2)}) copy-start(bf16[256,256]{1,0:T(8,128)(2,1)} %param.4) | copy-start | bytes 393220
  8.0 6.4 %copy-start.1 = (bf16[256,4096]{1,0:T(8,128)(2,1)S(1)}, bf16[256,4096]{1,0:T(8,128)(2,1)}, u32[]{:S(2)}) copy-start(bf16[256,4096]{1,0:T(8,128)(2,1)} %param.6) | copy-start | bytes 6291460
  8.0 511.2 %all-reduce.3.cloned.1.call-start = ((), (), s32[]{:S(2)}) async-start(), calls=%async_computation.2 | async-start | bytes 262144 | tf_op jit(solution)/shard_map/psum | solution.py:83
  266.2 44.6 %copy-start = (bf16[256,256]{1,0:T(8,128)(2,1)S(1)}, bf16[256,256]{1,0:T(8,128)(2,1)}, u32[]{:S(2)}) copy-start(bf16[256,256]{1,0:T(8,128)(2,1)} %param.5) | copy-start | bytes 393220
  266.2 44.7 %copy-start.2 = (bf16[256,4096]{1,0:T(8,128)(2,1)S(1)}, bf16[256,4096]{1,0:T(8,128)(2,1)}, u32[]{:S(2)}) copy-start(bf16[256,4096]{1,0:T(8,128)(2,1)} %param.7) | copy-start | bytes 6291460
  390.6 4.9 copy-start.3
  396.9 125.1 %reduce-scatter.2.cloned.1.call-start = ((), (), s32[]{:S(2)}) async-start(), calls=%async_computation.1 | async-start | bytes 2228224 | tf_op jit(solution)/shard_map/reduce_scatter | solution.py:73
Sparse Core Ops, SparseCore 0:
  397.0 122.0 all-reduce.2
Sparse Core Ops, SparseCore 1:
  400.8 54.4 reduce-scatter.1
where the time goes:
time: 530 us; the launch traced here: 529 us
  blocking collectives  357 us (67%)
  waiting for transfers between devices  120 us (23%)
  other arithmetic  27.2 us (5%)
  between operations  15.6 us (3%)
  matrix products  9.75 us (2%)
    psum x3, blocking collectives, shards(): lax.psum(jnp.sum(teacher_exp * proto_scale[None, :], axis=1), 'proto')  229 us
    psum x3, blocking collectives, proto_update(): sums = lax.psum(jnp.sum(teacher_exp * crop_scale[:, None], axis=0), 'batch')  127 us
    psum x1, waiting for transfers between devices, shards(): lax.psum(local_grad.astype(jnp.bfloat16), 'proto').astype(jnp.float32)  120 us
  transfers between devices with their start and end apart: 2, of which 1 were waited for; matrix products, arithmetic and copies ran while one was open for 1% of the time, Pallas kernels for 0%

commit v1 on v0

v1 whole, which is shorter than its diff:
```python
import functools
import math

import jax
import jax.numpy as jnp
from jax import lax
from jax.experimental import pallas as pl
from jax.experimental.pallas import tpu as pltpu
from jax.sharding import PartitionSpec as P

ITERS = 3
TEACHER_TEMP = 0.07
STUDENT_TEMP = 0.1
EPSILON = 1e-06
MESH = pl.DeviceIdType.MESH

NZ = 16
NJ = 32
D = 256
B = 256
C = 4096
PROTOS = C * NJ
CROPS = B * NZ
LANES = 128
TILES = C // LANES
WIDE = 256
WTILES = C // WIDE
ROWS = D // NZ
SUBS = 4
SUB = C // SUBS
STEPS = NZ // 2
FROWS = B // NJ


def kernel(
    tf_ref, sf_ref, tw_ref, sw_ref, wout_ref, fout_ref,
    e_ref, s_ref, ws_ref, wpart_ref, ring_ref,
    zt_ref, zs_ref, zst_ref, zfull_ref, zlen_ref,
    pr_ref, pf_ref, psend_ref, pbuf_ref, u_ref, crep_ref, srep_ref,
    csend_ref, cbuf_ref, ssend_ref, sbuf_ref,
    fsend_ref, fbuf_ref, gsend_ref, gbuf_ref,
    psend_sem, precv_sem, csend_sem, crecv_sem, ssend_sem, srecv_sem,
    fsend_sem, frecv_sem, gsend_sem, grecv_sem, wsend_sem, wrecv_sem,
):
    z = lax.axis_index("batch")
    j = lax.axis_index("proto")

    def zpeer(k):
        return (lax.rem(z + k, NZ), j)

    def jpeer(k):
        return (z, lax.rem(j + k, NJ))

    barrier = pltpu.get_barrier_semaphore()
    for k in range(1, NJ):
        pl.semaphore_signal(barrier, 1, device_id=jpeer(k), device_id_type=MESH)
    for k in range(1, NZ):
        pl.semaphore_signal(barrier, 1, device_id=zpeer(k), device_id_type=MESH)

    tf = tf_ref[...].astype(jnp.float32)
    tlen = jnp.sqrt(jnp.sum(tf * tf, axis=1, keepdims=True) + EPSILON)
    zt_ref[...] = (tf / tlen).astype(jnp.bfloat16)

    def columns(t):
        return pl.ds(pl.multiple_of(t * WIDE, WIDE), WIDE)

    def unit_columns(raw):
        values = raw.astype(jnp.float32)
        length = jnp.sqrt(jnp.sum(values * values, axis=0, keepdims=True) + EPSILON)
        return (values / length).astype(jnp.bfloat16)

    def teacher_tile(t, carry):
        wt = unit_columns(tw_ref[:, columns(t)])
        dots = jnp.dot(zt_ref[...], wt, preferred_element_type=jnp.float32)
        e = jnp.exp(dots * (1.0 / TEACHER_TEMP))
        e_ref[2 * t] = e[:, :LANES]
        e_ref[2 * t + 1] = e[:, LANES:]
        pr_ref[t] = jnp.sum(e, axis=0, keepdims=True)
        return carry

    lax.fori_loop(0, WTILES, teacher_tile, 0)

    def send_protos(it):
        pf_ref[...] = jnp.concatenate([pr_ref[t] for t in range(WTILES)], axis=0)
        psend_ref[it] = pf_ref[...].astype(jnp.bfloat16)
        for k in range(1, NZ):
            pltpu.make_async_remote_copy(
                src_ref=psend_ref.at[it],
                dst_ref=pbuf_ref.at[it, k - 1],
                send_sem=psend_sem.at[it],
                recv_sem=precv_sem.at[it],
                device_id=zpeer(k),
                device_id_type=MESH,
            ).start()

    def receive_protos(it):
        whole = pbuf_ref.at[it]
        pltpu.make_async_copy(whole, whole, precv_sem.at[it]).wait()
        total = pf_ref[...]
        for k in range(NZ - 1):
            total = total + pbuf_ref[it, k].astype(jnp.float32)
        scale = 1.0 / total
        for t in range(WTILES):
            u_ref[t] = scale[t:t + 1]

    pl.semaphore_wait(barrier, NJ + NZ - 2)
    send_protos(0)

    sf = sf_ref[...].astype(jnp.float32)
    slen = jnp.sqrt(jnp.sum(sf * sf, axis=1, keepdims=True) + EPSILON)
    sfull = sf / slen
    zfull_ref[...] = sfull
    zlen_ref[...] = jnp.broadcast_to(slen, (B, LANES))
    zs_ref[...] = sfull.astype(jnp.bfloat16)
    zst_ref[...] = jnp.transpose(sfull).astype(jnp.bfloat16)

    def student_tile(t, acc):
        ws = unit_columns(sw_ref[:, columns(t)])
        ws_ref[:, columns(t)] = ws
        dots = jnp.dot(zs_ref[...], ws, preferred_element_type=jnp.float32)
        s = jnp.exp(dots * (1.0 / STUDENT_TEMP))
        s_ref[2 * t] = s[:, :LANES]
        s_ref[2 * t + 1] = s[:, LANES:]
        return acc + s[:, :LANES] + s[:, LANES:]

    sacc = lax.fori_loop(0, WTILES, student_tile, jnp.zeros((B, LANES), jnp.float32))
    ssend_ref[...] = jnp.sum(jnp.transpose(sacc), axis=0, keepdims=True)
    for k in range(1, NJ):
        pltpu.make_async_remote_copy(
            src_ref=ssend_ref,
            dst_ref=sbuf_ref.at[k - 1],
            send_sem=ssend_sem,
            recv_sem=srecv_sem,
            device_id=jpeer(k),
            device_id_type=MESH,
        ).start()

    for it in range(ITERS):
        if it > 0:
            def proto_tile(t, carry):
                c = crep_ref[...]
                for h in range(2):
                    pr_ref[t, :, h * LANES:(h + 1) * LANES] = jnp.sum(
                        e_ref[2 * t + h] * c, axis=0, keepdims=True
                    )
                return carry

            lax.fori_loop(0, WTILES, proto_tile, 0)
            send_protos(it)
        receive_protos(it)
        last = it == ITERS - 1

        def crop_tile(t, acc):
            for h in range(2):
                scaled = e_ref[2 * t + h] * u_ref[t, :, h * LANES:(h + 1) * LANES]
                if last:
                    e_ref[2 * t + h] = scaled
                acc = acc + scaled
            return acc

        acc = lax.fori_loop(0, WTILES, crop_tile, jnp.zeros((B, LANES), jnp.float32))
        row = jnp.sum(jnp.transpose(acc), axis=0, keepdims=True)
        csend_ref[it] = row
        for k in range(1, NJ):
            pltpu.make_async_remote_copy(
                src_ref=csend_ref.at[it],
                dst_ref=cbuf_ref.at[it, k - 1],
                send_sem=csend_sem.at[it],
                recv_sem=crecv_sem.at[it],
                device_id=jpeer(k),
                device_id_type=MESH,
            ).start()
        got = cbuf_ref.at[it]
        pltpu.make_async_copy(got, got, crecv_sem.at[it]).wait()
        for k in range(NJ - 1):
            row = row + cbuf_ref[it, k]
        crop_scale = 1.0 / row
        if last:
            crop_scale = crop_scale * float(PROTOS)
        crep_ref[...] = jnp.transpose(jnp.broadcast_to(crop_scale, (LANES, B)))

    pltpu.make_async_copy(sbuf_ref, sbuf_ref, srecv_sem).wait()
    row = ssend_ref[...]
    for k in range(NJ - 1):
        row = row + sbuf_ref[k]
    inverse = float(PROTOS) / row
    srep_ref[...] = jnp.transpose(jnp.broadcast_to(inverse, (LANES, B)))
    weight_factor = math.sqrt(D / CROPS)
    feature_factor = math.sqrt(D / PROTOS)

    def grad_tile(t, acc):
        c = crep_ref[...]
        halves = [s_ref[2 * t + h] * srep_ref[...] - e_ref[2 * t + h] * c for h in range(2)]
        grad = jnp.concatenate([half.astype(jnp.bfloat16) for half in halves], axis=1)
        term = jnp.dot(zst_ref[...], grad, preferred_element_type=jnp.float32)
        wpart_ref[:, columns(t)] = (term * weight_factor).astype(jnp.bfloat16)
        return acc + lax.dot_general(
            grad, ws_ref[:, columns(t)], (((1,), (1,)), ((), ())), preferred_element_type=jnp.float32
        )

    feature = lax.fori_loop(0, WTILES, grad_tile, jnp.zeros((B, D), jnp.float32))

    def chunk(distance, sub):
        target = lax.rem(z + distance, NZ)
        return wpart_ref.at[pl.ds(pl.multiple_of(target * ROWS, ROWS), ROWS), pl.ds(sub * SUB, SUB)]

    def subs_of(way, step):
        half = SUBS // 2
        if step > 0:
            return tuple(range(SUBS))
        return tuple(range(half)) if way == 0 else tuple(range(half, SUBS))

    def ring_copy(way, step, sub):
        distance = STEPS - step if way == 0 else NZ - (STEPS - step)
        return pltpu.make_async_remote_copy(
            src_ref=chunk(distance, sub),
            dst_ref=ring_ref.at[way, step, :, pl.ds(sub * SUB, SUB)],
            send_sem=wsend_sem.at[way, step, sub],
            recv_sem=wrecv_sem.at[way, step, sub],
            device_id=zpeer(1 if way == 0 else NZ - 1),
            device_id_type=MESH,
        )

    def ring_step(step):
        for sub in range(SUBS):
            for way in range(2):
                if sub not in subs_of(way, step):
                    continue
                copy = ring_copy(way, step, sub)
                if step > 0 and sub in subs_of(way, step - 1):
                    ring_copy(way, step - 1, sub).wait_recv()
                    distance = STEPS - step if way == 0 else NZ - (STEPS - step)
                    own = chunk(distance, sub)
                    arrived = ring_ref[way, step - 1, :, sub * SUB:(sub + 1) * SUB]
                    own[...] = (own[...].astype(jnp.float32) + arrived.astype(jnp.float32)).astype(jnp.bfloat16)
                copy.start()

    ring_step(0)

    feature = feature * feature_factor
    for i in range(NJ):
        rows = feature[i * FROWS:(i + 1) * FROWS]
        fsend_ref[i] = jnp.concatenate([rows[:, :LANES], rows[:, LANES:]], axis=0).astype(jnp.bfloat16)
    for k in range(1, NJ):
        pltpu.make_async_remote_copy(
            src_ref=fsend_ref.at[lax.rem(j + k, NJ)],
            dst_ref=fbuf_ref.at[k - 1],
            send_sem=fsend_sem,
            recv_sem=frecv_sem,
            device_id=jpeer(k),
            device_id_type=MESH,
        ).start()

    ring_step(1)
    ring_step(2)

    whole = fbuf_ref
    pltpu.make_async_copy(whole, whole, frecv_sem).wait()
    total = fsend_ref[j].astype(jnp.float32)
    for k in range(NJ - 1):
        total = total + fbuf_ref[k].astype(jnp.float32)
    unit_grad = jnp.concatenate([total[:FROWS], total[FROWS:]], axis=1)
    mine = pl.ds(pl.multiple_of(j * FROWS, FROWS), FROWS)
    unit = zfull_ref[mine, :]
    along = jnp.sum(unit * unit_grad, axis=1, keepdims=True)
    length = zlen_ref[mine, :]
    rows = unit_grad - unit * along
    gsend_ref[...] = jnp.concatenate([rows[:, :LANES] / length, rows[:, LANES:] / length], axis=0).astype(jnp.bfloat16)
    for k in range(1, NJ):
        pltpu.make_async_remote_copy(
            src_ref=gsend_ref,
            dst_ref=gbuf_ref.at[j],
            send_sem=gsend_sem,
            recv_sem=grecv_sem,
            device_id=jpeer(k),
            device_id_type=MESH,
        ).start()
    gbuf_ref[j] = gsend_ref[...]

    for step in range(3, STEPS):
        ring_step(step)

    got = gbuf_ref.at[pl.ds(0, NJ - 1)]
    pltpu.make_async_copy(got, got, grecv_sem).wait()
    for i in range(NJ // 2):
        one = gbuf_ref[2 * i].astype(jnp.float32)
        two = gbuf_ref[2 * i + 1].astype(jnp.float32)
        left = jnp.concatenate([one[:FROWS], two[:FROWS]], axis=0)
        right = jnp.concatenate([one[FROWS:], two[FROWS:]], axis=0)
        fout_ref[2 * FROWS * i:2 * FROWS * (i + 1), :] = jnp.concatenate([left, right], axis=1).astype(jnp.bfloat16)

    for sub in range(SUBS):
        at = pl.ds(sub * SUB, SUB)
        total = chunk(0, sub)[...].astype(jnp.float32)
        for way in range(2):
            ring_copy(way, STEPS - 1, sub).wait_recv()
            total = total + ring_ref[way, STEPS - 1, :, at].astype(jnp.float32)
        wout_ref[:, at] = total.astype(jnp.bfloat16)

    for it in range(ITERS):
        whole = pbuf_ref.at[it]
        pltpu.make_async_copy(whole, whole, psend_sem.at[it]).wait()
        got = cbuf_ref.at[it]
        pltpu.make_async_copy(got, got, csend_sem.at[it]).wait()
    pltpu.make_async_copy(sbuf_ref, sbuf_ref, ssend_sem).wait()
    pltpu.make_async_copy(fbuf_ref, fbuf_ref, fsend_sem).wait()
    pltpu.make_async_copy(fbuf_ref, fbuf_ref, gsend_sem).wait()
    for step in range(STEPS):
        for way in range(2):
            for sub in subs_of(way, step):
                ring_copy(way, step, sub).wait_send()


def shards(teacher_feats, student_feats, teacher_weight, student_weight):
    f32, bf16 = jnp.float32, jnp.bfloat16
    vmem, dma = pltpu.VMEM, pltpu.SemaphoreType.DMA
    scratch = [
        vmem((TILES, B, LANES), f32),
        vmem((TILES, B, LANES), f32),
        vmem((D, C), bf16),
        vmem((D, C), bf16),
        vmem((2, STEPS, ROWS, C), bf16),
        vmem((B, D), bf16),
        vmem((B, D), bf16),
        vmem((D, B), bf16),
        vmem((B, D), f32),
        vmem((B, LANES), f32),
        vmem((WTILES, 1, WIDE), f32),
        vmem((WTILES, WIDE), f32),
        vmem((ITERS, WTILES, WIDE), bf16),
        vmem((ITERS, NZ - 1, WTILES, WIDE), bf16),
        vmem((WTILES, 1, WIDE), f32),
        vmem((B, LANES), f32),
        vmem((B, LANES), f32),
        vmem((ITERS, 1, B), f32),
        vmem((ITERS, NJ - 1, 1, B), f32),
        vmem((1, B), f32),
        vmem((NJ - 1, 1, B), f32),
        vmem((NJ, 2 * FROWS, LANES), bf16),
        vmem((NJ - 1, 2 * FROWS, LANES), bf16),
        vmem((2 * FROWS, LANES), bf16),
        vmem((NJ, 2 * FROWS, LANES), bf16),
        dma((ITERS,)), dma((ITERS,)), dma((ITERS,)), dma((ITERS,)), dma, dma,
        dma, dma, dma, dma, dma((2, STEPS, SUBS)), dma((2, STEPS, SUBS)),
    ]
    return pl.pallas_call(
        kernel,
        out_shape=(jax.ShapeDtypeStruct((ROWS, C), bf16), jax.ShapeDtypeStruct((B, D), bf16)),
        in_specs=[pl.BlockSpec(memory_space=pltpu.VMEM)] * 4,
        out_specs=(pl.BlockSpec(memory_space=pltpu.VMEM), pl.BlockSpec(memory_space=pltpu.VMEM)),
        scratch_shapes=scratch,
        compiler_params=pltpu.CompilerParams(
            collective_id=0, has_side_effects=True, vmem_limit_bytes=48 << 20
        ),
        cost_estimate=pl.CostEstimate(
            flops=8 * B * C * D, bytes_accessed=4 * D * C + 6 * B * D, transcendentals=2 * B * C
        ),
    )(teacher_feats, student_feats, teacher_weight, student_weight)


def solution(mesh):
    return jax.shard_map(
        shards,
        mesh=mesh,
        in_specs=(P("batch", None), P("batch", None), P(None, "proto"), P(None, "proto")),
        out_specs=(P("batch", "proto"), P("batch", None)),
        check_vma=False,
    )
```

time: 530 us -> 109 us (0.21)
  the two profiles are of different devices: /device:TPU:1 before, /device:TPU:8 now
where the time goes in v1:
time: 109 us
  Pallas kernels  102 us (94%)
  local copies, waits for them, and re-layouts  6.29 us (6%)
    pallas_call x1, Pallas kernels, shards(): pl.pallas_call(kernel, out_shape=(jax.ShapeDtypeStruct((ROWS, C), bf16),...  102 us
    unnamed x10, local copies, waits for them, and re-layouts  6.29 us

profile of v1, /device:TPU:8, one launch (start us, length us, event | category | flops | bytes accessed | tf_op | source)
XLA Modules:
  0.0 109.0 jit_solution(2585129388151917752)
XLA Ops:
  0.6 0.0 copy-start
  0.6 1.6 %copy-done = bf16[256,4096]{1,0:T(8,128)(2,1)S(1)} copy-done((bf16[256,4096]{1,0:T(8,128)(2,1)S(1)}, bf16[256,4096]{1,0:T(8,128)(2,1)}, u32[]{:S(2)}) %copy-start) | copy-done | bytes 2097176
  2.2 0.0 copy-start.1
  2.2 1.6 %copy-done.1 = bf16[256,4096]{1,0:T(8,128)(2,1)S(1)} copy-done((bf16[256,4096]{1,0:T(8,128)(2,1)S(1)}, bf16[256,4096]{1,0:T(8,128)(2,1)}, u32[]{:S(2)}) %copy-start.1) | copy-done | bytes 2097176
  3.8 0.0 copy-start.2
  3.8 0.9 copy-done.2
  4.7 0.0 copy-start.3
  4.7 0.9 copy-done.3
  5.6 102.0 %shard_map.59 = (bf16[16,4096]{1,0:T(8,128)(2,1)S(1)}, bf16[256,256]{1,0:T(8,128)(2,1)S(1)}) custom-call(bf16[256,256]{1,0:T(8,128)(2,1)S(1)} %copy-done.2, bf16[256,256]{1,0:T(8,128)(2,1)S(1)} %copy-done.3, bf16[256,4096]{1,0:T(8,128)(2,1)S(1)} %copy-done, bf16[256,4096]{1,0:T(8,128)(2,1)S(1)} %copy-done.1), custom_call_target="tpu_custom_call" | custom-call | flops 2147483648 | bytes 4587520 | tf_op jit(solution)/shard_map/pallas_call | solution.py:346
  107.7 0.7 copy.8
  108.3 0.7 copy.9
Async XLA Ops:
  0.6 1.6 %copy-start = (bf16[256,4096]{1,0:T(8,128)(2,1)S(1)}, bf16[256,4096]{1,0:T(8,128)(2,1)}, u32[]{:S(2)}) copy-start(bf16[256,4096]{1,0:T(8,128)(2,1)} %tw_ref.1) | copy-start | bytes 6291460
  2.2 1.6 %copy-start.1 = (bf16[256,4096]{1,0:T(8,128)(2,1)S(1)}, bf16[256,4096]{1,0:T(8,128)(2,1)}, u32[]{:S(2)}) copy-start(bf16[256,4096]{1,0:T(8,128)(2,1)} %sw_ref.1) | copy-start | bytes 6291460
  3.8 0.9 copy-start.2
  4.7 0.9 copy-start.3

commit v2 on v1

--- a/solution.py
+++ b/solution.py
@@ -25,22 +25,26 @@
 TILES = C // LANES
 WIDE = 256
 WTILES = C // WIDE
+PARTS = 4
+PART = C // PARTS
 ROWS = D // NZ
 SUBS = 4
 SUB = C // SUBS
 STEPS = NZ // 2
 FROWS = B // NJ
+Z_ORDER = sorted(range(1, NZ), key=lambda k: -min(k, NZ - k))
 
 
 def kernel(
-    tf_ref, sf_ref, tw_ref, sw_ref, wout_ref, fout_ref,
-    e_ref, s_ref, ws_ref, wpart_ref, ring_ref,
+    tf_hbm, sf_hbm, tw_hbm, sw_hbm, wout_ref, fout_ref,
+    tf_ref, sf_ref, tw_ref, sw_ref,
+    e_ref, s_ref, ws_ref, grad_ref, wpart_ref, ring_ref,
     zt_ref, zs_ref, zst_ref, zfull_ref, zlen_ref,
     pr_ref, pf_ref, psend_ref, pbuf_ref, u_ref, crep_ref, srep_ref,
     csend_ref, cbuf_ref, ssend_ref, sbuf_ref,
     fsend_ref, fbuf_ref, gsend_ref, gbuf_ref,
     psend_sem, precv_sem, csend_sem, crecv_sem, ssend_sem, srecv_sem,
-    fsend_sem, frecv_sem, gsend_sem, grecv_sem, wsend_sem, wrecv_sem,
+    fsend_sem, frecv_sem, gsend_sem, grecv_sem, wsend_sem, wrecv_sem, load_sem, tload_sem,
 ):
     z = lax.axis_index("batch")
     j = lax.axis_index("proto")
@@ -54,36 +58,51 @@
     barrier = pltpu.get_barrier_semaphore()
     for k in range(1, NJ):
         pl.semaphore_signal(barrier, 1, device_id=jpeer(k), device_id_type=MESH)
-    for k in range(1, NZ):
+    for k in Z_ORDER:
         pl.semaphore_signal(barrier, 1, device_id=zpeer(k), device_id_type=MESH)
 
+    load_tf = pltpu.make_async_copy(tf_hbm, tf_ref, load_sem.at[0])
+    load_sf = pltpu.make_async_copy(sf_hbm, sf_ref, load_sem.at[1])
+    load_sw = pltpu.make_async_copy(sw_hbm, sw_ref, load_sem.at[2])
+
+    def load_tw(part):
+        at = pl.ds(pl.multiple_of(part * PART, PART), PART)
+        return pltpu.make_async_copy(tw_hbm.at[:, at], tw_ref.at[:, at], tload_sem.at[part])
+
+    load_tf.start()
+    for part in range(PARTS):
+        load_tw(part).start()
+    load_sf.start()
+    load_sw.start()
+    load_tf.wait()
+
     tf = tf_ref[...].astype(jnp.float32)
-    tlen = jnp.sqrt(jnp.sum(tf * tf, axis=1, keepdims=True) + EPSILON)
-    zt_ref[...] = (tf / tlen).astype(jnp.bfloat16)
+    zt_ref[...] = (tf * lax.rsqrt(jnp.sum(tf * tf, axis=1, keepdims=True) + EPSILON)).astype(jnp.bfloat16)
 
     def columns(t):
         return pl.ds(pl.multiple_of(t * WIDE, WIDE), WIDE)
 
-    def unit_columns(raw):
-        values = raw.astype(jnp.float32)
-        length = jnp.sqrt(jnp.sum(values * values, axis=0, keepdims=True) + EPSILON)
-        return (values / length).astype(jnp.bfloat16)
+    def inverse_lengths(values):
+        return lax.rsqrt(jnp.sum(values * values, axis=0, keepdims=True) + EPSILON)
 
     def teacher_tile(t, carry):
-        wt = unit_columns(tw_ref[:, columns(t)])
-        dots = jnp.dot(zt_ref[...], wt, preferred_element_type=jnp.float32)
-        e = jnp.exp(dots * (1.0 / TEACHER_TEMP))
+        raw = tw_ref[:, columns(t)]
+        scale = inverse_lengths(raw.astype(jnp.float32)) * (1.0 / TEACHER_TEMP)
+        dots = jnp.dot(zt_ref[...], raw, preferred_element_type=jnp.float32)
+        e = jnp.exp(dots * scale)
         e_ref[2 * t] = e[:, :LANES]
         e_ref[2 * t + 1] = e[:, LANES:]
         pr_ref[t] = jnp.sum(e, axis=0, keepdims=True)
         return carry
 
-    lax.fori_loop(0, WTILES, teacher_tile, 0)
+    for part in range(PARTS):
+        load_tw(part).wait()
+        lax.fori_loop(part * (WTILES // PARTS), (part + 1) * (WTILES // PARTS), teacher_tile, 0, unroll=True)
 
     def send_protos(it):
         pf_ref[...] = jnp.concatenate([pr_ref[t] for t in range(WTILES)], axis=0)
         psend_ref[it] = pf_ref[...].astype(jnp.bfloat16)
-        for k in range(1, NZ):
+        for k in Z_ORDER:
             pltpu.make_async_remote_copy(
                 src_ref=psend_ref.at[it],
                 dst_ref=pbuf_ref.at[it, k - 1],
@@ -106,6 +125,8 @@
     pl.semaphore_wait(barrier, NJ + NZ - 2)
     send_protos(0)
 
+    load_sf.wait()
+    load_sw.wait()
     sf = sf_ref[...].astype(jnp.float32)
     slen = jnp.sqrt(jnp.sum(sf * sf, axis=1, keepdims=True) + EPSILON)
     sfull = sf / slen
@@ -115,7 +136,8 @@
     zst_ref[...] = jnp.transpose(sfull).astype(jnp.bfloat16)
 
     def student_tile(t, acc):
-        ws = unit_columns(sw_ref[:, columns(t)])
+        values = sw_ref[:, columns(t)].astype(jnp.float32)
+        ws = (values * inverse_lengths(values)).astype(jnp.bfloat16)
         ws_ref[:, columns(t)] = ws
         dots = jnp.dot(zs_ref[...], ws, preferred_element_type=jnp.float32)
         s = jnp.exp(dots * (1.0 / STUDENT_TEMP))
@@ -123,7 +145,7 @@
         s_ref[2 * t + 1] = s[:, LANES:]
         return acc + s[:, :LANES] + s[:, LANES:]
 
-    sacc = lax.fori_loop(0, WTILES, student_tile, jnp.zeros((B, LANES), jnp.float32))
+    sacc = lax.fori_loop(0, WTILES, student_tile, jnp.zeros((B, LANES), jnp.float32), unroll=2)
     ssend_ref[...] = jnp.sum(jnp.transpose(sacc), axis=0, keepdims=True)
     for k in range(1, NJ):
         pltpu.make_async_remote_copy(
@@ -137,15 +159,20 @@
 
     for it in range(ITERS):
         if it > 0:
-            def proto_tile(t, carry):
-                c = crep_ref[...]
-                for h in range(2):
-                    pr_ref[t, :, h * LANES:(h + 1) * LANES] = jnp.sum(
-                        e_ref[2 * t + h] * c, axis=0, keepdims=True
+            def proto_tiles(g, carry):
+                totals = [None] * 4
+                for r in range(0, B, 8):
+                    c = crep_ref[r:r + 8]
+                    for i in range(4):
+                        term = e_ref[4 * g + i, r:r + 8] * c
+                        totals[i] = term if r == 0 else totals[i] + term
+                for i in range(4):
+                    pr_ref[2 * g + i // 2, :, (i % 2) * LANES:(i % 2 + 1) * LANES] = jnp.sum(
+                        totals[i], axis=0, keepdims=True
                     )
                 return carry
 
-            lax.fori_loop(0, WTILES, proto_tile, 0)
+            lax.fori_loop(0, TILES // 4, proto_tiles, 0, unroll=2)
             send_protos(it)
         receive_protos(it)
         last = it == ITERS - 1
@@ -158,7 +185,7 @@
                 acc = acc + scaled
             return acc
 
-        acc = lax.fori_loop(0, WTILES, crop_tile, jnp.zeros((B, LANES), jnp.float32))
+        acc = lax.fori_loop(0, WTILES, crop_tile, jnp.zeros((B, LANES), jnp.float32), unroll=4)
         row = jnp.sum(jnp.transpose(acc), axis=0, keepdims=True)
         csend_ref[it] = row
         for k in range(1, NJ):
@@ -188,17 +215,16 @@
     weight_factor = math.sqrt(D / CROPS)
     feature_factor = math.sqrt(D / PROTOS)
 
-    def grad_tile(t, acc):
+    def grad_tile(t, carry):
         c = crep_ref[...]
         halves = [s_ref[2 * t + h] * srep_ref[...] - e_ref[2 * t + h] * c for h in range(2)]
         grad = jnp.concatenate([half.astype(jnp.bfloat16) for half in halves], axis=1)
         term = jnp.dot(zst_ref[...], grad, preferred_element_type=jnp.float32)
         wpart_ref[:, columns(t)] = (term * weight_factor).astype(jnp.bfloat16)
-        return acc + lax.dot_general(
-            grad, ws_ref[:, columns(t)], (((1,), (1,)), ((), ())), preferred_element_type=jnp.float32
-        )
-
-    feature = lax.fori_loop(0, WTILES, grad_tile, jnp.zeros((B, D), jnp.float32))
+        grad_ref[:, columns(t)] = grad
+        return carry
+
+    lax.fori_loop(0, WTILES, grad_tile, 0, unroll=4)
 
     def chunk(distance, sub):
         target = lax.rem(z + distance, NZ)
@@ -237,7 +263,9 @@
 
     ring_step(0)
 
-    feature = feature * feature_factor
+    feature = lax.dot_general(
+        grad_ref[...], ws_ref[...], (((1,), (1,)), ((), ())), preferred_element_type=jnp.float32
+    ) * feature_factor
     for i in range(NJ):
         rows = feature[i * FROWS:(i + 1) * FROWS]
         fsend_ref[i] = jnp.concatenate([rows[:, :LANES], rows[:, LANES:]], axis=0).astype(jnp.bfloat16)
@@ -315,9 +343,14 @@
     f32, bf16 = jnp.float32, jnp.bfloat16
     vmem, dma = pltpu.VMEM, pltpu.SemaphoreType.DMA
     scratch = [
+        vmem((B, D), bf16),
+        vmem((B, D), bf16),
+        vmem((D, C), bf16),
+        vmem((D, C), bf16),
         vmem((TILES, B, LANES), f32),
         vmem((TILES, B, LANES), f32),
         vmem((D, C), bf16),
+        vmem((B, C), bf16),
         vmem((D, C), bf16),
         vmem((2, STEPS, ROWS, C), bf16),
         vmem((B, D), bf16),
@@ -341,16 +374,16 @@
         vmem((2 * FROWS, LANES), bf16),
         vmem((NJ, 2 * FROWS, LANES), bf16),
         dma((ITERS,)), dma((ITERS,)), dma((ITERS,)), dma((ITERS,)), dma, dma,
-        dma, dma, dma, dma, dma((2, STEPS, SUBS)), dma((2, STEPS, SUBS)),
+        dma, dma, dma, dma, dma((2, STEPS, SUBS)), dma((2, STEPS, SUBS)), dma((3,)), dma((PARTS,)),
     ]
     return pl.pallas_call(
         kernel,
         out_shape=(jax.ShapeDtypeStruct((ROWS, C), bf16), jax.ShapeDtypeStruct((B, D), bf16)),
-        in_specs=[pl.BlockSpec(memory_space=pltpu.VMEM)] * 4,
+        in_specs=[pl.BlockSpec(memory_space=pltpu.HBM)] * 4,
         out_specs=(pl.BlockSpec(memory_space=pltpu.VMEM), pl.BlockSpec(memory_space=pltpu.VMEM)),
         scratch_shapes=scratch,
         compiler_params=pltpu.CompilerParams(
-            collective_id=0, has_side_effects=True, vmem_limit_bytes=48 << 20
+            collective_id=0, has_side_effects=True, vmem_limit_bytes=(536 << 20) // 10
         ),
         cost_estimate=pl.CostEstimate(
             flops=8 * B * C * D, bytes_accessed=4 * D * C + 6 * B * D, transcendentals=2 * B * C

time: 109 us -> 94.7 us (0.87)
  the two profiles are of different devices: /device:TPU:8 before, /device:TPU:32 now
where the time goes in v2:
time: 94.7 us; the launch traced here: 94.6 us
  Pallas kernels  92.7 us (98%)
  local copies, waits for them, and re-layouts  1.31 us (1%)
    pallas_call x1, Pallas kernels, shards(): pl.pallas_call(kernel, out_shape=(jax.ShapeDtypeStruct((ROWS, C), bf16),...  92.7 us

profile of v2, /device:TPU:32, one launch (start us, length us, event | category | flops | bytes accessed | tf_op | source)
XLA Modules:
  0.0 94.6 jit_solution(5088060276963694016)
XLA Ops:
  0.6 92.7 %shard_map.59 = (bf16[16,4096]{1,0:T(8,128)(2,1)S(1)}, bf16[256,256]{1,0:T(8,128)(2,1)S(1)}) custom-call(bf16[256,256]{1,0:T(8,128)(2,1)} %tf_hbm.1, bf16[256,256]{1,0:T(8,128)(2,1)} %sf_hbm.1, bf16[256,4096]{1,0:T(8,128)(2,1)} %tw_hbm.1, bf16[256,4096]{1,0:T(8,128)(2,1)} %sw_hbm.1), custom_call_target="tpu_custom_call" | custom-call | flops 2147483648 | bytes 4587520 | tf_op jit(solution)/shard_map/pallas_call | solution.py:379
  93.3 0.7 copy.8
  94.0 0.7 copy.9

commit v3 on v2

--- a/solution.py
+++ b/solution.py
@@ -28,9 +28,9 @@
 PARTS = 4
 PART = C // PARTS
 ROWS = D // NZ
-SUBS = 4
-SUB = C // SUBS
-STEPS = NZ // 2
+NX, NY = 4, 4
+HALF = NZ // 2
+EARLY = 2
 FROWS = B // NJ
 Z_ORDER = sorted(range(1, NZ), key=lambda k: -min(k, NZ - k))
 
@@ -38,13 +38,15 @@
 def kernel(
     tf_hbm, sf_hbm, tw_hbm, sw_hbm, wout_ref, fout_ref,
     tf_ref, sf_ref, tw_ref, sw_ref,
-    e_ref, s_ref, ws_ref, grad_ref, wpart_ref, ring_ref,
-    zt_ref, zs_ref, zst_ref, zfull_ref, zlen_ref,
+    e_ref, s_ref, ws_ref, grad_ref, all_ref, we_ref, wsx_ref,
+    zt_ref, zs_ref, zfull_ref, zlen_ref,
+    twt_ref, swt_ref, tscale_ref, wacc_ref, wsend_ref, wrecv_ref, xsend_ref, xbuf_ref,
     pr_ref, pf_ref, psend_ref, pbuf_ref, u_ref, crep_ref, srep_ref,
     csend_ref, cbuf_ref, ssend_ref, sbuf_ref,
     fsend_ref, fbuf_ref, gsend_ref, gbuf_ref,
     psend_sem, precv_sem, csend_sem, crecv_sem, ssend_sem, srecv_sem,
-    fsend_sem, frecv_sem, gsend_sem, grecv_sem, wsend_sem, wrecv_sem, load_sem, tload_sem,
+    fsend_sem, frecv_sem, gsend_sem, grecv_sem, load_sem, tload_sem,
+    gather_send, gather_recv, xsend_sem, xrecv_sem, wsend_sem, wrecv_sem,
 ):
     z = lax.axis_index("batch")
     j = lax.axis_index("proto")
@@ -54,6 +56,16 @@
 
     def jpeer(k):
         return (z, lax.rem(j + k, NJ))
+
+    core = lax.rem(j, 2)
+    x = lax.rem(j // 2, NX)
+    y = j // (2 * NX)
+
+    def xpeer(k):
+        return (z, (y * NX + lax.rem(x + k, NX)) * 2 + core)
+
+    def ypeer(k):
+        return (z, (lax.rem(y + k, NY) * NX + x) * 2 + core)
 
     barrier = pltpu.get_barrier_semaphore()
     for k in range(1, NJ):
@@ -133,7 +145,6 @@
     zfull_ref[...] = sfull
     zlen_ref[...] = jnp.broadcast_to(slen, (B, LANES))
     zs_ref[...] = sfull.astype(jnp.bfloat16)
-    zst_ref[...] = jnp.transpose(sfull).astype(jnp.bfloat16)
 
     def student_tile(t, acc):
         values = sw_ref[:, columns(t)].astype(jnp.float32)
@@ -156,6 +167,60 @@
             device_id=jpeer(k),
             device_id_type=MESH,
         ).start()
+
+    def post(src, dst, stage, peer):
+        pltpu.make_async_remote_copy(
+            src_ref=src,
+            dst_ref=dst,
+            send_sem=gather_send.at[stage],
+            recv_sem=gather_recv.at[stage],
+            device_id=peer,
+            device_id_type=MESH,
+        ).start()
+
+    def arrived(stage, amount):
+        pltpu.make_async_copy(amount, amount, gather_recv.at[stage]).wait()
+
+    amounts = (
+        all_ref.at[0, pl.ds(0, NZ - 1), 0, 0],
+        all_ref.at[0, pl.ds(0, HALF), 0, pl.ds(0, NX - 1)],
+        all_ref.at[0, pl.ds(0, HALF), 0, pl.ds(0, NX - 1)],
+        all_ref.at[0, pl.ds(0, EARLY), pl.ds(0, NY - 1)],
+        all_ref.at[0, pl.ds(0, EARLY), pl.ds(0, NY - 1)],
+        all_ref.at[0, pl.ds(0, HALF - EARLY), pl.ds(0, NY - 1)],
+        all_ref.at[0, pl.ds(0, HALF - EARLY), pl.ds(0, NY - 1)],
+        all_ref.at[0],
+    )
+    first, second = pl.ds(0, HALF), pl.ds(HALF, HALF)
+
+    def gather_z():
+        rows = pl.ds(pl.multiple_of((j // 2) * ROWS, ROWS), ROWS)
+        both = jnp.where(core == 0, zt_ref[rows, :].astype(jnp.float32), zs_ref[rows, :].astype(jnp.float32))
+        all_ref[core, z, y, x] = both.astype(jnp.bfloat16)
+        mine = all_ref.at[core, z, y, x]
+        for k in Z_ORDER:
+            post(mine, mine, 0, zpeer(k))
+
+    def gather_one():
+        arrived(0, amounts[0])
+        for k in (2, 1, 3):
+            one = all_ref.at[core, first, y, x]
+            post(one, one, 1, xpeer(k))
+            two = all_ref.at[core, second, y, x]
+            post(two, two, 2, ypeer(k))
+
+    def gather_two(begin, end, stage):
+        for k in (2, 1, 3):
+            one = all_ref.at[core, pl.ds(begin, end - begin), y]
+            post(one, one, stage, ypeer(k))
+            two = all_ref.at[core, pl.ds(HALF + begin, end - begin), :, x]
+            post(two, two, stage + 1, xpeer(k))
+
+    def gather_core():
+        mine = all_ref.at[core]
+        post(mine, mine, 7, (z, j + 1 - 2 * core))
+
+    gather_z()
 
     for it in range(ITERS):
         if it > 0:
@@ -174,6 +239,21 @@
 
             lax.fori_loop(0, TILES // 4, proto_tiles, 0, unroll=2)
             send_protos(it)
+        if it == 1:
+            gather_one()
+            own = columns(z)
+            raw = jnp.transpose(tw_ref[:, own].astype(jnp.float32))
+            twt_ref[...] = raw.astype(jnp.bfloat16)
+            scale = lax.rsqrt(jnp.sum(raw * raw, axis=1, keepdims=True) + EPSILON) * (1.0 / TEACHER_TEMP)
+            tscale_ref[...] = jnp.broadcast_to(scale, (WIDE, LANES))
+            swt_ref[...] = jnp.transpose(ws_ref[:, own].astype(jnp.float32)).astype(jnp.bfloat16)
+            arrived(1, amounts[1])
+            arrived(2, amounts[2])
+            gather_two(0, EARLY, 3)
+        if it == 2:
+            arrived(3, amounts[3])
+            arrived(4, amounts[4])
+            gather_two(EARLY, HALF, 5)
         receive_protos(it)
         last = it == ITERS - 1
 
@@ -197,6 +277,10 @@
                 device_id=jpeer(k),
                 device_id_type=MESH,
             ).start()
+        if last:
+            arrived(5, amounts[5])
+            arrived(6, amounts[6])
+            gather_core()
         got = cbuf_ref.at[it]
         pltpu.make_async_copy(got, got, crecv_sem.at[it]).wait()
         for k in range(NJ - 1):
@@ -204,6 +288,7 @@
         crop_scale = 1.0 / row
         if last:
             crop_scale = crop_scale * float(PROTOS)
+            xsend_ref[:, :B] = crop_scale
         crep_ref[...] = jnp.transpose(jnp.broadcast_to(crop_scale, (LANES, B)))
 
     pltpu.make_async_copy(sbuf_ref, sbuf_ref, srecv_sem).wait()
@@ -211,6 +296,16 @@
     for k in range(NJ - 1):
         row = row + sbuf_ref[k]
     inverse = float(PROTOS) / row
+    xsend_ref[:, B:] = inverse
+    for k in Z_ORDER:
+        pltpu.make_async_remote_copy(
+            src_ref=xsend_ref,
+            dst_ref=xbuf_ref.at[k - 1],
+            send_sem=xsend_sem,
+            recv_sem=xrecv_sem.at[k - 1],
+            device_id=zpeer(k),
+            device_id_type=MESH,
+        ).start()
     srep_ref[...] = jnp.transpose(jnp.broadcast_to(inverse, (LANES, B)))
     weight_factor = math.sqrt(D / CROPS)
     feature_factor = math.sqrt(D / PROTOS)
@@ -219,49 +314,10 @@
         c = crep_ref[...]
         halves = [s_ref[2 * t + h] * srep_ref[...] - e_ref[2 * t + h] * c for h in range(2)]
         grad = jnp.concatenate([half.astype(jnp.bfloat16) for half in halves], axis=1)
-        term = jnp.dot(zst_ref[...], grad, preferred_element_type=jnp.float32)
-        wpart_ref[:, columns(t)] = (term * weight_factor).astype(jnp.bfloat16)
         grad_ref[:, columns(t)] = grad
         return carry
 
     lax.fori_loop(0, WTILES, grad_tile, 0, unroll=4)
-
-    def chunk(distance, sub):
-        target = lax.rem(z + distance, NZ)
-        return wpart_ref.at[pl.ds(pl.multiple_of(target * ROWS, ROWS), ROWS), pl.ds(sub * SUB, SUB)]
-
-    def subs_of(way, step):
-        half = SUBS // 2
-        if step > 0:
-            return tuple(range(SUBS))
-        return tuple(range(half)) if way == 0 else tuple(range(half, SUBS))
-
-    def ring_copy(way, step, sub):
-        distance = STEPS - step if way == 0 else NZ - (STEPS - step)
-        return pltpu.make_async_remote_copy(
-            src_ref=chunk(distance, sub),
-            dst_ref=ring_ref.at[way, step, :, pl.ds(sub * SUB, SUB)],
-            send_sem=wsend_sem.at[way, step, sub],
-            recv_sem=wrecv_sem.at[way, step, sub],
-            device_id=zpeer(1 if way == 0 else NZ - 1),
-            device_id_type=MESH,
-        )
-
-    def ring_step(step):
-        for sub in range(SUBS):
-            for way in range(2):
-                if sub not in subs_of(way, step):
-                    continue
-                copy = ring_copy(way, step, sub)
-                if step > 0 and sub in subs_of(way, step - 1):
-                    ring_copy(way, step - 1, sub).wait_recv()
-                    distance = STEPS - step if way == 0 else NZ - (STEPS - step)
-                    own = chunk(distance, sub)
-                    arrived = ring_ref[way, step - 1, :, sub * SUB:(sub + 1) * SUB]
-                    own[...] = (own[...].astype(jnp.float32) + arrived.astype(jnp.float32)).astype(jnp.bfloat16)
-                copy.start()
-
-    ring_step(0)
 
     feature = lax.dot_general(
         grad_ref[...], ws_ref[...], (((1,), (1,)), ((), ())), preferred_element_type=jnp.float32
@@ -279,8 +335,44 @@
             device_id_type=MESH,
         ).start()
 
-    ring_step(1)
-    ring_step(2)
+    arrived(7, amounts[7])
+    ucol = jnp.transpose(jnp.broadcast_to(u_ref[z], (LANES, WIDE)))
+
+    def own_tile(b, carry):
+        zt = all_ref[0, b].reshape(B, D)
+        zs = all_ref[1, b].reshape(B, D)
+        contract = (((1,), (1,)), ((), ()))
+        dots = lax.dot_general(twt_ref[...], zt, contract, preferred_element_type=jnp.float32)
+        logits = lax.dot_general(swt_ref[...], zs, contract, preferred_element_type=jnp.float32)
+        for h in range(2):
+            at = slice(h * LANES, (h + 1) * LANES)
+            we_ref[b, :, at] = jnp.exp(dots[:, at] * tscale_ref[...]) * ucol
+        wsx_ref[b] = jnp.exp(logits * (1.0 / STUDENT_TEMP))
+        return carry
+
+    lax.fori_loop(0, NZ, own_tile, 0, unroll=2)
+
+    def block(b, scales):
+        grad = (wsx_ref[b] * scales[:, B:] - we_ref[b] * scales[:, :B]).astype(jnp.bfloat16)
+        return jnp.dot(grad, all_ref[1, b].reshape(B, D), preferred_element_type=jnp.float32)
+
+    wacc_ref[...] = block(z, xsend_ref[...])
+    for k in reversed(Z_ORDER):
+        slot = xbuf_ref.at[k - 1]
+        pltpu.make_async_copy(slot, slot, xrecv_sem.at[k - 1]).wait()
+        wacc_ref[...] += block(lax.rem(z + NZ - k, NZ), xbuf_ref[k - 1])
+    weight = (jnp.transpose(wacc_ref[...]) * weight_factor).astype(jnp.bfloat16)
+    for b in range(NZ):
+        wsend_ref[b] = weight[b * ROWS:(b + 1) * ROWS]
+    for k in Z_ORDER:
+        pltpu.make_async_remote_copy(
+            src_ref=wsend_ref.at[lax.rem(z + k, NZ)],
+            dst_ref=wrecv_ref.at[k - 1],
+            send_sem=wsend_sem,
+            recv_sem=wrecv_sem,
+            device_id=zpeer(k),
+            device_id_type=MESH,
+        ).start()
 
     whole = fbuf_ref
     pltpu.make_async_copy(whole, whole, frecv_sem).wait()
@@ -305,9 +397,6 @@
         ).start()
     gbuf_ref[j] = gsend_ref[...]
 
-    for step in range(3, STEPS):
-        ring_step(step)
-
     got = gbuf_ref.at[pl.ds(0, NJ - 1)]
     pltpu.make_async_copy(got, got, grecv_sem).wait()
     for i in range(NJ // 2):
@@ -317,13 +406,10 @@
         right = jnp.concatenate([one[FROWS:], two[FROWS:]], axis=0)
         fout_ref[2 * FROWS * i:2 * FROWS * (i + 1), :] = jnp.concatenate([left, right], axis=1).astype(jnp.bfloat16)
 
-    for sub in range(SUBS):
-        at = pl.ds(sub * SUB, SUB)
-        total = chunk(0, sub)[...].astype(jnp.float32)
-        for way in range(2):
-            ring_copy(way, STEPS - 1, sub).wait_recv()
-            total = total + ring_ref[way, STEPS - 1, :, at].astype(jnp.float32)
-        wout_ref[:, at] = total.astype(jnp.bfloat16)
+    pltpu.make_async_copy(wrecv_ref, wrecv_ref, wrecv_sem).wait()
+    wout_ref[:, columns(z)] = wsend_ref[z]
+    for k in range(1, NZ):
+        wout_ref[:, columns(lax.rem(z + NZ - k, NZ))] = wrecv_ref[k - 1]
 
     for it in range(ITERS):
         whole = pbuf_ref.at[it]
@@ -333,10 +419,10 @@
     pltpu.make_async_copy(sbuf_ref, sbuf_ref, ssend_sem).wait()
     pltpu.make_async_copy(fbuf_ref, fbuf_ref, fsend_sem).wait()
     pltpu.make_async_copy(fbuf_ref, fbuf_ref, gsend_sem).wait()
-    for step in range(STEPS):
-        for way in range(2):
-            for sub in subs_of(way, step):
-                ring_copy(way, step, sub).wait_send()
+    pltpu.make_async_copy(xbuf_ref, xbuf_ref, xsend_sem).wait()
+    pltpu.make_async_copy(wrecv_ref, wrecv_ref, wsend_sem).wait()
+    for stage in range(len(amounts)):
+        pltpu.make_async_copy(amounts[stage], amounts[stage], gather_send.at[stage]).wait()
 
 
 def shards(teacher_feats, student_feats, teacher_weight, student_weight):
@@ -351,13 +437,21 @@
         vmem((TILES, B, LANES), f32),
         vmem((D, C), bf16),
         vmem((B, C), bf16),
-        vmem((D, C), bf16),
-        vmem((2, STEPS, ROWS, C), bf16),
+        vmem((2, NZ, NY, NX, ROWS, D), bf16),
+        vmem((NZ, WIDE, B), f32),
+        vmem((NZ, WIDE, B), f32),
         vmem((B, D), bf16),
         vmem((B, D), bf16),
-        vmem((D, B), bf16),
         vmem((B, D), f32),
         vmem((B, LANES), f32),
+        vmem((WIDE, D), bf16),
+        vmem((WIDE, D), bf16),
+        vmem((WIDE, LANES), f32),
+        vmem((WIDE, D), f32),
+        vmem((NZ, ROWS, WIDE), bf16),
+        vmem((NZ - 1, ROWS, WIDE), bf16),
+        vmem((1, 2 * B), f32),
+        vmem((NZ - 1, 1, 2 * B), f32),
         vmem((WTILES, 1, WIDE), f32),
         vmem((WTILES, WIDE), f32),
         vmem((ITERS, WTILES, WIDE), bf16),
@@ -374,7 +468,8 @@
         vmem((2 * FROWS, LANES), bf16),
         vmem((NJ, 2 * FROWS, LANES), bf16),
         dma((ITERS,)), dma((ITERS,)), dma((ITERS,)), dma((ITERS,)), dma, dma,
-        dma, dma, dma, dma, dma((2, STEPS, SUBS)), dma((2, STEPS, SUBS)), dma((3,)), dma((PARTS,)),
+        dma, dma, dma, dma, dma((3,)), dma((PARTS,)),
+        dma((8,)), dma((8,)), dma, dma((NZ - 1,)), dma, dma,
     ]
     return pl.pallas_call(
         kernel,

time: 94.7 us -> 80.4 us (0.85)
  the two profiles are of different devices: /device:TPU:32 before, /device:TPU:1 now
where the time goes in v3:
time: 80.4 us; the launch traced here: 80.3 us
  Pallas kernels  78.4 us (98%)
  local copies, waits for them, and re-layouts  1.31 us (2%)
    pallas_call x1, Pallas kernels, shards(): pl.pallas_call(kernel, out_shape=(jax.ShapeDtypeStruct((ROWS, C), bf16),...  78.4 us

profile of v3, /device:TPU:1, one launch (start us, length us, event | category | flops | bytes accessed | tf_op | source)
XLA Modules:
  0.0 80.3 jit_solution(18339046879042817438)
XLA Ops:
  0.6 78.4 %shard_map.59 = (bf16[16,4096]{1,0:T(8,128)(2,1)S(1)}, bf16[256,256]{1,0:T(8,128)(2,1)S(1)}) custom-call(bf16[256,256]{1,0:T(8,128)(2,1)} %tf_hbm.1, bf16[256,256]{1,0:T(8,128)(2,1)} %sf_hbm.1, bf16[256,4096]{1,0:T(8,128)(2,1)} %tw_hbm.1, bf16[256,4096]{1,0:T(8,128)(2,1)} %sw_hbm.1), custom_call_target="tpu_custom_call" | custom-call | flops 2147483648 | bytes 4587520 | tf_op jit(solution)/shard_map/pallas_call | solution.py:474
  79.0 0.7 copy.8
  79.7 0.7 copy.9

commit v4 on v3

--- a/solution.py
+++ b/solution.py
@@ -23,6 +23,7 @@
 CROPS = B * NZ
 LANES = 128
 TILES = C // LANES
+HTILES = TILES // 2
 WIDE = 256
 WTILES = C // WIDE
 PARTS = 4
@@ -30,7 +31,7 @@
 ROWS = D // NZ
 NX, NY = 4, 4
 HALF = NZ // 2
-EARLY = 2
+EARLY = 3
 FROWS = B // NJ
 Z_ORDER = sorted(range(1, NZ), key=lambda k: -min(k, NZ - k))
 
@@ -39,8 +40,8 @@
     tf_hbm, sf_hbm, tw_hbm, sw_hbm, wout_ref, fout_ref,
     tf_ref, sf_ref, tw_ref, sw_ref,
     e_ref, s_ref, ws_ref, grad_ref, all_ref, we_ref, wsx_ref,
-    zt_ref, zs_ref, zfull_ref, zlen_ref,
-    twt_ref, swt_ref, tscale_ref, wacc_ref, wsend_ref, wrecv_ref, xsend_ref, xbuf_ref,
+    zt_ref, zs_ref, ztt_ref, zst_ref, zfull_ref, zlen_ref,
+    twt_ref, swt_ref, tscale_ref, ucol_ref, wacc_ref, wsend_ref, wrecv_ref, xsend_ref, xbuf_ref,
     pr_ref, pf_ref, psend_ref, pbuf_ref, u_ref, crep_ref, srep_ref,
     csend_ref, cbuf_ref, ssend_ref, sbuf_ref,
     fsend_ref, fbuf_ref, gsend_ref, gbuf_ref,
@@ -68,10 +69,10 @@
         return (z, (lax.rem(y + k, NY) * NX + x) * 2 + core)
 
     barrier = pltpu.get_barrier_semaphore()
+    for k in Z_ORDER:
+        pl.semaphore_signal(barrier, 1, device_id=zpeer(k), device_id_type=MESH)
     for k in range(1, NJ):
         pl.semaphore_signal(barrier, 1, device_id=jpeer(k), device_id_type=MESH)
-    for k in Z_ORDER:
-        pl.semaphore_signal(barrier, 1, device_id=zpeer(k), device_id_type=MESH)
 
     load_tf = pltpu.make_async_copy(tf_hbm, tf_ref, load_sem.at[0])
     load_sf = pltpu.make_async_copy(sf_hbm, sf_ref, load_sem.at[1])
@@ -104,7 +105,9 @@
         e = jnp.exp(dots * scale)
         e_ref[2 * t] = e[:, :LANES]
         e_ref[2 * t + 1] = e[:, LANES:]
-        pr_ref[t] = jnp.sum(e, axis=0, keepdims=True)
+        sums = jnp.sum(e, axis=0, keepdims=True)
+        pr_ref[2 * t] = sums[:, :LANES]
+        pr_ref[2 * t + 1] = sums[:, LANES:]
         return carry
 
     for part in range(PARTS):
@@ -112,27 +115,30 @@
         lax.fori_loop(part * (WTILES // PARTS), (part + 1) * (WTILES // PARTS), teacher_tile, 0, unroll=True)
 
     def send_protos(it):
-        pf_ref[...] = jnp.concatenate([pr_ref[t] for t in range(WTILES)], axis=0)
-        psend_ref[it] = pf_ref[...].astype(jnp.bfloat16)
+        for part in range(2):
+            sums = jnp.concatenate([pr_ref[part * HTILES + t] for t in range(HTILES)], axis=0)
+            pf_ref[part] = sums
+            psend_ref[it, part] = sums.astype(jnp.bfloat16)
         for k in Z_ORDER:
-            pltpu.make_async_remote_copy(
-                src_ref=psend_ref.at[it],
-                dst_ref=pbuf_ref.at[it, k - 1],
-                send_sem=psend_sem.at[it],
-                recv_sem=precv_sem.at[it],
-                device_id=zpeer(k),
-                device_id_type=MESH,
-            ).start()
-
-    def receive_protos(it):
-        whole = pbuf_ref.at[it]
-        pltpu.make_async_copy(whole, whole, precv_sem.at[it]).wait()
-        total = pf_ref[...]
+            for part in range(2):
+                pltpu.make_async_remote_copy(
+                    src_ref=psend_ref.at[it, part],
+                    dst_ref=pbuf_ref.at[it, part, k - 1],
+                    send_sem=psend_sem.at[it, part],
+                    recv_sem=precv_sem.at[it, part],
+                    device_id=zpeer(k),
+                    device_id_type=MESH,
+                ).start()
+
+    def receive_protos(it, part):
+        whole = pbuf_ref.at[it, part]
+        pltpu.make_async_copy(whole, whole, precv_sem.at[it, part]).wait()
+        total = pf_ref[part]
         for k in range(NZ - 1):
-            total = total + pbuf_ref[it, k].astype(jnp.float32)
+            total = total + pbuf_ref[it, part, k].astype(jnp.float32)
         scale = 1.0 / total
-        for t in range(WTILES):
-            u_ref[t] = scale[t:t + 1]
+        for t in range(HTILES):
+            u_ref[part * HTILES + t] = scale[t:t + 1]
 
     pl.semaphore_wait(barrier, NJ + NZ - 2)
     send_protos(0)
@@ -189,14 +195,18 @@
         all_ref.at[0, pl.ds(0, EARLY), pl.ds(0, NY - 1)],
         all_ref.at[0, pl.ds(0, HALF - EARLY), pl.ds(0, NY - 1)],
         all_ref.at[0, pl.ds(0, HALF - EARLY), pl.ds(0, NY - 1)],
-        all_ref.at[0],
+        all_ref.at[0, pl.ds(0, EARLY)],
+        all_ref.at[0, pl.ds(0, EARLY)],
+        all_ref.at[0, pl.ds(0, HALF - EARLY)],
+        all_ref.at[0, pl.ds(0, HALF - EARLY)],
     )
     first, second = pl.ds(0, HALF), pl.ds(HALF, HALF)
 
     def gather_z():
         rows = pl.ds(pl.multiple_of((j // 2) * ROWS, ROWS), ROWS)
-        both = jnp.where(core == 0, zt_ref[rows, :].astype(jnp.float32), zs_ref[rows, :].astype(jnp.float32))
-        all_ref[core, z, y, x] = both.astype(jnp.bfloat16)
+        ztt_ref[...] = jnp.transpose(zt_ref[...].astype(jnp.float32))
+        zst_ref[...] = jnp.transpose(zs_ref[...].astype(jnp.float32))
+        all_ref[core, z, y, x] = jnp.where(core == 0, ztt_ref[rows, :], zst_ref[rows, :]).astype(jnp.bfloat16)
         mine = all_ref.at[core, z, y, x]
         for k in Z_ORDER:
             post(mine, mine, 0, zpeer(k))
@@ -216,9 +226,42 @@
             two = all_ref.at[core, pl.ds(HALF + begin, end - begin), :, x]
             post(two, two, stage + 1, xpeer(k))
 
-    def gather_core():
-        mine = all_ref.at[core]
-        post(mine, mine, 7, (z, j + 1 - 2 * core))
+    def gather_core(begin, end, stage):
+        for half in range(2):
+            mine = all_ref.at[core, pl.ds(half * HALF + begin, end - begin)]
+            post(mine, mine, stage + half, (z, j + 1 - 2 * core))
+
+    def own_tile(b):
+        dots = jnp.dot(twt_ref[...], all_ref[0, b].reshape(D, B), preferred_element_type=jnp.float32)
+        logits = jnp.dot(swt_ref[...], all_ref[1, b].reshape(D, B), preferred_element_type=jnp.float32)
+        for h in range(2):
+            at = slice(h * LANES, (h + 1) * LANES)
+            we_ref[b, :, at] = jnp.exp(dots[:, at] * tscale_ref[...])
+        wsx_ref[b] = jnp.exp(logits * (1.0 / STUDENT_TEMP))
+
+    def own_tiles(begin, end, stage):
+        arrived(stage, amounts[stage])
+        arrived(stage + 1, amounts[stage + 1])
+
+        def pair(b, carry):
+            own_tile(b)
+            own_tile(HALF + b)
+            return carry
+
+        lax.fori_loop(begin, end, pair, 0)
+
+    def scale_own():
+        ucol_ref[...] = jnp.concatenate(
+            [jnp.transpose(jnp.broadcast_to(u_ref[2 * z + h], (LANES, LANES))) for h in range(2)], axis=0
+        )
+
+        def scaled(b, carry):
+            for h in range(2):
+                at = slice(h * LANES, (h + 1) * LANES)
+                we_ref[b, :, at] = we_ref[b, :, at] * ucol_ref[...]
+            return carry
+
+        lax.fori_loop(0, NZ, scaled, 0, unroll=2)
 
     gather_z()
 
@@ -232,9 +275,7 @@
                         term = e_ref[4 * g + i, r:r + 8] * c
                         totals[i] = term if r == 0 else totals[i] + term
                 for i in range(4):
-                    pr_ref[2 * g + i // 2, :, (i % 2) * LANES:(i % 2 + 1) * LANES] = jnp.sum(
-                        totals[i], axis=0, keepdims=True
-                    )
+                    pr_ref[4 * g + i] = jnp.sum(totals[i], axis=0, keepdims=True)
                 return carry
 
             lax.fori_loop(0, TILES // 4, proto_tiles, 0, unroll=2)
@@ -244,6 +285,13 @@
             own = columns(z)
             raw = jnp.transpose(tw_ref[:, own].astype(jnp.float32))
             twt_ref[...] = raw.astype(jnp.bfloat16)
+            pltpu.make_async_copy(sbuf_ref, sbuf_ref, srecv_sem).wait()
+            student = ssend_ref[...]
+            for k in range(NJ - 1):
+                student = student + sbuf_ref[k]
+            inverse = float(PROTOS) / student
+            xsend_ref[:, B:] = inverse
+            srep_ref[...] = jnp.transpose(jnp.broadcast_to(inverse, (LANES, B)))
             scale = lax.rsqrt(jnp.sum(raw * raw, axis=1, keepdims=True) + EPSILON) * (1.0 / TEACHER_TEMP)
             tscale_ref[...] = jnp.broadcast_to(scale, (WIDE, LANES))
             swt_ref[...] = jnp.transpose(ws_ref[:, own].astype(jnp.float32)).astype(jnp.bfloat16)
@@ -254,18 +302,20 @@
             arrived(3, amounts[3])
             arrived(4, amounts[4])
             gather_two(EARLY, HALF, 5)
-        receive_protos(it)
+            gather_core(0, EARLY, 7)
+            own_tiles(0, EARLY, 7)
         last = it == ITERS - 1
 
         def crop_tile(t, acc):
-            for h in range(2):
-                scaled = e_ref[2 * t + h] * u_ref[t, :, h * LANES:(h + 1) * LANES]
-                if last:
-                    e_ref[2 * t + h] = scaled
-                acc = acc + scaled
-            return acc
-
-        acc = lax.fori_loop(0, WTILES, crop_tile, jnp.zeros((B, LANES), jnp.float32), unroll=4)
+            scaled = e_ref[t] * u_ref[t]
+            if last:
+                e_ref[t] = scaled
+            return acc + scaled
+
+        acc = jnp.zeros((B, LANES), jnp.float32)
+        for part in range(2):
+            receive_protos(it, part)
+            acc = lax.fori_loop(part * HTILES, (part + 1) * HTILES, crop_tile, acc, unroll=4)
         row = jnp.sum(jnp.transpose(acc), axis=0, keepdims=True)
         csend_ref[it] = row
         for k in range(1, NJ):
@@ -280,7 +330,7 @@
         if last:
             arrived(5, amounts[5])
             arrived(6, amounts[6])
-            gather_core()
+            gather_core(EARLY, HALF, 9)
         got = cbuf_ref.at[it]
         pltpu.make_async_copy(got, got, crecv_sem.at[it]).wait()
         for k in range(NJ - 1):
@@ -289,24 +339,17 @@
         if last:
             crop_scale = crop_scale * float(PROTOS)
             xsend_ref[:, :B] = crop_scale
+            for k in Z_ORDER:
+                pltpu.make_async_remote_copy(
+                    src_ref=xsend_ref,
+                    dst_ref=xbuf_ref.at[k - 1],
+                    send_sem=xsend_sem,
+                    recv_sem=xrecv_sem.at[k - 1],
+                    device_id=zpeer(k),
+                    device_id_type=MESH,
+                ).start()
         crep_ref[...] = jnp.transpose(jnp.broadcast_to(crop_scale, (LANES, B)))
 
-    pltpu.make_async_copy(sbuf_ref, sbuf_ref, srecv_sem).wait()
-    row = ssend_ref[...]
-    for k in range(NJ - 1):
-        row = row + sbuf_ref[k]
-    inverse = float(PROTOS) / row
-    xsend_ref[:, B:] = inverse
-    for k in Z_ORDER:
-        pltpu.make_async_remote_copy(
-            src_ref=xsend_ref,
-            dst_ref=xbuf_ref.at[k - 1],
-            send_sem=xsend_sem,
-            recv_sem=xrecv_sem.at[k - 1],
-            device_id=zpeer(k),
-            device_id_type=MESH,
-        ).start()
-    srep_ref[...] = jnp.transpose(jnp.broadcast_to(inverse, (LANES, B)))
     weight_factor = math.sqrt(D / CROPS)
     feature_factor = math.sqrt(D / PROTOS)
 
@@ -335,33 +378,24 @@
             device_id_type=MESH,
         ).start()
 
-    arrived(7, amounts[7])
-    ucol = jnp.transpose(jnp.broadcast_to(u_ref[z], (LANES, WIDE)))
-
-    def own_tile(b, carry):
-        zt = all_ref[0, b].reshape(B, D)
-        zs = all_ref[1, b].reshape(B, D)
-        contract = (((1,), (1,)), ((), ()))
-        dots = lax.dot_general(twt_ref[...], zt, contract, preferred_element_type=jnp.float32)
-        logits = lax.dot_general(swt_ref[...], zs, contract, preferred_element_type=jnp.float32)
-        for h in range(2):
-            at = slice(h * LANES, (h + 1) * LANES)
-            we_ref[b, :, at] = jnp.exp(dots[:, at] * tscale_ref[...]) * ucol
-        wsx_ref[b] = jnp.exp(logits * (1.0 / STUDENT_TEMP))
-        return carry
-
-    lax.fori_loop(0, NZ, own_tile, 0, unroll=2)
-
+    own_tiles(EARLY, HALF, 9)
+    scale_own()
     def block(b, scales):
         grad = (wsx_ref[b] * scales[:, B:] - we_ref[b] * scales[:, :B]).astype(jnp.bfloat16)
-        return jnp.dot(grad, all_ref[1, b].reshape(B, D), preferred_element_type=jnp.float32)
-
-    wacc_ref[...] = block(z, xsend_ref[...])
-    for k in reversed(Z_ORDER):
-        slot = xbuf_ref.at[k - 1]
-        pltpu.make_async_copy(slot, slot, xrecv_sem.at[k - 1]).wait()
-        wacc_ref[...] += block(lax.rem(z + NZ - k, NZ), xbuf_ref[k - 1])
-    weight = (jnp.transpose(wacc_ref[...]) * weight_factor).astype(jnp.bfloat16)
+        return lax.dot_general(
+            all_ref[1, b].reshape(D, B), grad, (((1,), (1,)), ((), ())), preferred_element_type=jnp.float32
+        )
+
+    near = Z_ORDER[::-1]
+    for group in (near[:4], near[4:8], near[8:12], near[12:14], near[14:]):
+        for k in group:
+            slot = xbuf_ref.at[k - 1]
+            pltpu.make_async_copy(slot, slot, xrecv_sem.at[k - 1]).wait()
+        total = block(z, xsend_ref[...]) if group[0] == near[0] else wacc_ref[...]
+        for k in group:
+            total = total + block(lax.rem(z + NZ - k, NZ), xbuf_ref[k - 1])
+        wacc_ref[...] = total
+    weight = (wacc_ref[...] * weight_factor).astype(jnp.bfloat16)
     for b in range(NZ):
         wsend_ref[b] = weight[b * ROWS:(b + 1) * ROWS]
     for k in Z_ORDER:
@@ -406,23 +440,24 @@
         right = jnp.concatenate([one[FROWS:], two[FROWS:]], axis=0)
         fout_ref[2 * FROWS * i:2 * FROWS * (i + 1), :] = jnp.concatenate([left, right], axis=1).astype(jnp.bfloat16)
 
-    pltpu.make_async_copy(wrecv_ref, wrecv_ref, wrecv_sem).wait()
-    wout_ref[:, columns(z)] = wsend_ref[z]
-    for k in range(1, NZ):
-        wout_ref[:, columns(lax.rem(z + NZ - k, NZ))] = wrecv_ref[k - 1]
-
     for it in range(ITERS):
-        whole = pbuf_ref.at[it]
-        pltpu.make_async_copy(whole, whole, psend_sem.at[it]).wait()
+        for part in range(2):
+            whole = pbuf_ref.at[it, part]
+            pltpu.make_async_copy(whole, whole, psend_sem.at[it, part]).wait()
         got = cbuf_ref.at[it]
         pltpu.make_async_copy(got, got, csend_sem.at[it]).wait()
     pltpu.make_async_copy(sbuf_ref, sbuf_ref, ssend_sem).wait()
     pltpu.make_async_copy(fbuf_ref, fbuf_ref, fsend_sem).wait()
     pltpu.make_async_copy(fbuf_ref, fbuf_ref, gsend_sem).wait()
     pltpu.make_async_copy(xbuf_ref, xbuf_ref, xsend_sem).wait()
-    pltpu.make_async_copy(wrecv_ref, wrecv_ref, wsend_sem).wait()
     for stage in range(len(amounts)):
         pltpu.make_async_copy(amounts[stage], amounts[stage], gather_send.at[stage]).wait()
+
+    pltpu.make_async_copy(wrecv_ref, wrecv_ref, wrecv_sem).wait()
+    wout_ref[:, columns(z)] = wsend_ref[z]
+    for k in range(1, NZ):
+        wout_ref[:, columns(lax.rem(z + NZ - k, NZ))] = wrecv_ref[k - 1]
+    pltpu.make_async_copy(wrecv_ref, wrecv_ref, wsend_sem).wait()
 
 
 def shards(teacher_feats, student_feats, teacher_weight, student_weight):
@@ -442,21 +477,24 @@
         vmem((NZ, WIDE, B), f32),
         vmem((B, D), bf16),
         vmem((B, D), bf16),
+        vmem((D, B), f32),
+        vmem((D, B), f32),
         vmem((B, D), f32),
         vmem((B, LANES), f32),
         vmem((WIDE, D), bf16),
         vmem((WIDE, D), bf16),
         vmem((WIDE, LANES), f32),
-        vmem((WIDE, D), f32),
+        vmem((WIDE, LANES), f32),
+        vmem((D, WIDE), f32),
         vmem((NZ, ROWS, WIDE), bf16),
         vmem((NZ - 1, ROWS, WIDE), bf16),
         vmem((1, 2 * B), f32),
         vmem((NZ - 1, 1, 2 * B), f32),
-        vmem((WTILES, 1, WIDE), f32),
-        vmem((WTILES, WIDE), f32),
-        vmem((ITERS, WTILES, WIDE), bf16),
-        vmem((ITERS, NZ - 1, WTILES, WIDE), bf16),
-        vmem((WTILES, 1, WIDE), f32),
+        vmem((TILES, 1, LANES), f32),
+        vmem((2, HTILES, LANES), f32),
+        vmem((ITERS, 2, HTILES, LANES), bf16),
+        vmem((ITERS, 2, NZ - 1, HTILES, LANES), bf16),
+        vmem((TILES, 1, LANES), f32),
         vmem((B, LANES), f32),
         vmem((B, LANES), f32),
         vmem((ITERS, 1, B), f32),
@@ -467,9 +505,9 @@
         vmem((NJ - 1, 2 * FROWS, LANES), bf16),
         vmem((2 * FROWS, LANES), bf16),
         vmem((NJ, 2 * FROWS, LANES), bf16),
-        dma((ITERS,)), dma((ITERS,)), dma((ITERS,)), dma((ITERS,)), dma, dma,
+        dma((ITERS, 2)), dma((ITERS, 2)), dma((ITERS,)), dma((ITERS,)), dma, dma,
         dma, dma, dma, dma, dma((3,)), dma((PARTS,)),
-        dma((8,)), dma((8,)), dma, dma((NZ - 1,)), dma, dma,
+        dma((11,)), dma((11,)), dma, dma((NZ - 1,)), dma, dma,
     ]
     return pl.pallas_call(
         kernel,

time: 80.4 us -> 78.7 us (0.979)
  Pallas kernels: 78.4 us -> 75.9 us
    pallas_call x1, Pallas kernels: 78.4 us -> 75.9 us  [shards(): pl.pallas_call(kernel, out_shape=(jax.ShapeDtypeStruct((ROWS, C), bf16),...]
where the time goes in v4:
time: 78.7 us; the launch traced here: 77.8 us
  Pallas kernels  75.9 us (96%)
  local copies, waits for them, and re-layouts  1.31 us (2%)
    pallas_call x1, Pallas kernels, shards(): pl.pallas_call(kernel, out_shape=(jax.ShapeDtypeStruct((ROWS, C), bf16),...  75.9 us

profile of v4, /device:TPU:1, one launch (start us, length us, event | category | flops | bytes accessed | tf_op | source)
XLA Modules:
  0.0 77.8 jit_solution(7700529668677897391)
XLA Ops:
  0.6 75.9 %shard_map.59 = (bf16[16,4096]{1,0:T(8,128)(2,1)S(1)}, bf16[256,256]{1,0:T(8,128)(2,1)S(1)}) custom-call(bf16[256,256]{1,0:T(8,128)(2,1)} %tf_hbm.1, bf16[256,256]{1,0:T(8,128)(2,1)} %sf_hbm.1, bf16[256,4096]{1,0:T(8,128)(2,1)} %tw_hbm.1, bf16[256,4096]{1,0:T(8,128)(2,1)} %sw_hbm.1), custom_call_target="tpu_custom_call" | custom-call | flops 2147483648 | bytes 4587520 | tf_op jit(solution)/shard_map/pallas_call | solution.py:512
  76.5 0.7 copy.8
  77.2 0.7 copy.9

commit v5 on v4

--- a/solution.py
+++ b/solution.py
@@ -34,6 +34,10 @@
 EARLY = 3
 FROWS = B // NJ
 Z_ORDER = sorted(range(1, NZ), key=lambda k: -min(k, NZ - k))
+PLANE = sorted(
+    ((dy, dx, dc) for dy in range(NY) for dx in range(NX) for dc in range(2) if dy or dx or dc),
+    key=lambda t: -(min(t[0], NY - t[0]) + min(t[1], NX - t[1])),
+)
 
 
 def kernel(
@@ -55,12 +59,16 @@
     def zpeer(k):
         return (lax.rem(z + k, NZ), j)
 
-    def jpeer(k):
-        return (z, lax.rem(j + k, NJ))
-
     core = lax.rem(j, 2)
     x = lax.rem(j // 2, NX)
     y = j // (2 * NX)
+
+    def jindex(k):
+        dy, dx, dc = PLANE[k - 1]
+        return (lax.rem(y + dy, NY) * NX + lax.rem(x + dx, NX)) * 2 + lax.rem(core + dc, 2)
+
+    def jpeer(k):
+        return (z, jindex(k))
 
     def xpeer(k):
         return (z, (y * NX + lax.rem(x + k, NX)) * 2 + core)
@@ -370,7 +378,7 @@
         fsend_ref[i] = jnp.concatenate([rows[:, :LANES], rows[:, LANES:]], axis=0).astype(jnp.bfloat16)
     for k in range(1, NJ):
         pltpu.make_async_remote_copy(
-            src_ref=fsend_ref.at[lax.rem(j + k, NJ)],
+            src_ref=fsend_ref.at[jindex(k)],
             dst_ref=fbuf_ref.at[k - 1],
             send_sem=fsend_sem,
             recv_sem=frecv_sem,

time: 78.7 us -> 78.5 us (level)
  no operation moved by 1% of the time
where the time goes in v5:
time: 78.5 us; the launch traced here: 77.7 us
  Pallas kernels  75.8 us (97%)
  local copies, waits for them, and re-layouts  1.31 us (2%)
    pallas_call x1, Pallas kernels, shards(): pl.pallas_call(kernel, out_shape=(jax.ShapeDtypeStruct((ROWS, C), bf16),...  75.8 us

profile of v5, /device:TPU:1, one launch (start us, length us, event | category | flops | bytes accessed | tf_op | source)
XLA Modules:
  0.0 77.7 jit_solution(6140959758645756892)
XLA Ops:
  0.6 75.8 %shard_map.59 = (bf16[16,4096]{1,0:T(8,128)(2,1)S(1)}, bf16[256,256]{1,0:T(8,128)(2,1)S(1)}) custom-call(bf16[256,256]{1,0:T(8,128)(2,1)} %tf_hbm.1, bf16[256,256]{1,0:T(8,128)(2,1)} %sf_hbm.1, bf16[256,4096]{1,0:T(8,128)(2,1)} %tw_hbm.1, bf16[256,4096]{1,0:T(8,128)(2,1)} %sw_hbm.1), custom_call_target="tpu_custom_call" | custom-call | flops 2147483648 | bytes 4587520 | tf_op jit(solution)/shard_map/pallas_call | solution.py:520
  76.4 0.7 copy.8
  77.0 0.7 copy.9
